TPU v7x, 512 devices: a whole 4x8x8 slice. The times are simulated.
512 devices in a mesh: grp: 8 (over x, core), dev: 64 (over z, y).
Axes of the slice: x: 4, y: 8, z: 8, core: 2. Of those that a mesh axis runs over, the one named last changes fastest.
Arguments:
- passages: bfloat16 [98304, 4096], P('dev'), may hold values from -6 to 6
- ckpt_weight: bfloat16 [4096, 4096], P('dev', 'grp'), may hold values from -0.09375 to 0.09375
- old_bank: bfloat16 [8192, 4096], P('dev', 'grp'), may hold values from -6 to 6
- touched: int32 [384], replicated, may hold values from 0 to 8191, as said below
- neg_owner: int32 [2048, 8], P('dev'), may hold values from 0 to 63, all different within a row; in each aligned block of 32 rows (0 to 31, 32 to 63, ...) at most 8 rows name the same one
- neg_row: int32 [2048, 8], P('dev'), may hold values from 0 to 127
- queries: bfloat16 [2048, 4096], P('dev', 'grp'), may hold values from -32 to 32
- positives: bfloat16 [2048, 4096], P('dev', 'grp'), may hold values from -64 to 64
Outputs:
- new_bank: bfloat16 [8192, 4096], P('dev', 'grp')
- losses: float32 [2048], P('dev')
- direction: float32 [2048, 4096], P('dev', 'grp')
Inputs may be any that keep to these rules, and one draw needn't show every extreme that they name: `touched`: distinct bank rows. `neg_owner`: the queries of one index of dev name one bank shard at most 8 times, a bound that some block reaches; a query names 8 different shards.
All inputs are finite; a program needn't handle non-finite values.
Results may differ from a plain program's by a relative error of at most 0.00046.
Values may be sent and summed in bfloat16 or wider, within the bound.
A program may use at most 64 MiB of HBM per device.

v0:
```python
import math

import jax
import jax.numpy as jnp
from jax import lax
from jax.sharding import PartitionSpec as P

D = 4096
PLEN = 256


def body(passages, ckpt_weight, old_bank, touched, neg_owner, neg_row, queries, positives):
    owner_index = lax.axis_index("dev")
    width_part = ckpt_weight.shape[1]
    bank_rows = old_bank.shape[0]
    token_rows = passages.shape[0]
    query_rows = queries.shape[0]
    per_query = neg_owner.shape[1]
    preact = jnp.dot(
        passages,
        lax.all_gather(ckpt_weight, "dev", axis=0, tiled=True),
        preferred_element_type=jnp.float32,
    )
    pooled = jnp.sum(jnp.tanh(preact).reshape(token_rows // PLEN, PLEN, width_part), axis=1)
    encoded = (pooled / math.sqrt(PLEN)).astype(jnp.bfloat16)
    all_encoded = lax.all_gather(encoded, "dev", axis=0, tiled=True)
    local_ids = touched - owner_index * bank_rows
    matches = (
        lax.broadcasted_iota(jnp.int32, (bank_rows, local_ids.shape[0]), 0) == local_ids[None, :]
    )
    placed = jnp.dot(
        matches.astype(jnp.bfloat16), all_encoded, preferred_element_type=jnp.float32
    ).astype(jnp.bfloat16)
    new_bank = jnp.where(jnp.any(matches, axis=1)[:, None], placed, old_bank)
    wanted_owner = neg_owner.reshape(-1)
    wanted_row = neg_row.reshape(-1)
    requests = wanted_owner.shape[0]
    global_ids = wanted_owner * bank_rows + wanted_row
    piece = lax.all_gather(new_bank, "dev", axis=0, tiled=True)
    inside = (global_ids >= 0) & (global_ids < piece.shape[0])
    rows_here = jnp.take(piece, jnp.clip(global_ids, 0, piece.shape[0] - 1), axis=0)
    negatives = jnp.where(
        inside[:, None], rows_here, jnp.zeros((requests, width_part), jnp.bfloat16)
    )
    key_rows = jnp.concatenate(
        [positives[:, None, :], negatives.reshape(query_rows, per_query, width_part)], axis=1
    )
    key_values = key_rows.astype(jnp.float32)
    query_values = queries.astype(jnp.float32)
    exact = lax.Precision.HIGHEST
    dot_sums = jnp.einsum("qd,qkd->qk", query_values, key_values, precision=exact)
    square_sums = jnp.einsum("qkd,qkd->qk", key_values, key_values, precision=exact)
    dot_sums, square_sums = lax.psum((dot_sums, square_sums), "grp")
    inverse = lax.rsqrt(square_sums / D + 1e-06)
    scores = dot_sums * inverse / math.sqrt(D)
    highest = jnp.max(scores, axis=1, keepdims=True)
    weights = jnp.exp(scores - highest)
    summed = jnp.sum(weights, axis=1, keepdims=True)
    probs = weights / summed
    losses = highest[:, 0] + jnp.log(summed[:, 0]) - scores[:, 0]
    target = (lax.broadcasted_iota(jnp.int32, (1, per_query + 1), 1) == 0).astype(jnp.float32)
    coefficient = (probs - target) * inverse
    direction = jnp.einsum("qk,qkd->qd", coefficient, key_values, precision=exact)
    return (new_bank, losses, direction)


def solution(mesh):
    return jax.shard_map(
        body,
        mesh=mesh,
        in_specs=(
            P("dev", None),
            P("dev", "grp"),
            P("dev", "grp"),
            P(),
            P("dev", None),
            P("dev", None),
            P("dev", "grp"),
            P("dev", "grp"),
        ),
        out_specs=(P("dev", "grp"), P("dev"), P("dev", "grp")),
        check_vma=False,
    )
```

profile of v0, /device:TPU:1, one launch (start us, length us, event | category | flops | bytes accessed | tf_op | source)
XLA Modules:
  0.0 298.4 jit_solution(9848145081466698026)
XLA Ops:
  7.2 0.0 copy-start
  7.2 0.0 all-gather.4.cloned.1.call-start
  7.2 0.7 all-gather.4.cloned.1.call-update
  7.9 0.0 all-gather.6.cloned.1.call-start
  8.0 0.7 broadcast_subtract_fusion
  8.7 0.1 fusion.5
  8.8 91.1 %all-gather.4.cloned.1.call-done = bf16[4096,512]{1,0:T(8,128)(2,1)} async-done(((bf16[64,512]{1,0:T(8,128)(2,1)}), bf16[4096,512]{1,0:T(8,128)(2,1)}) %all-gather.4.cloned.1.call-update) | async-done | bytes 4194320 | tf_op jit(solution)/shard_map/all_gather | solution.py:21
  99.8 10.5 %convolution_tanh_fusion = f32[1536,512]{1,0:T(8,128)S(1)} fusion(bf16[1536,4096]{1,0:T(8,128)(2,1)} %param.8, bf16[4096,512]{1,0:T(8,128)(2,1)} %all-gather.4.cloned.1.call-done), kind=kOutput, calls=%fused_computation.1 | convolution fusion | flops 6442450944 | bytes 19922944 | tf_op jit(solution)/shard_map/dot_general | solution.py:19
  110.4 0.0 copy-start.1
  110.4 0.3 reduce_sum.18
  110.7 36.1 %all-gather = bf16[64,6,512]{2,1,0:T(8,128)(2,1)S(1)} all-gather(bf16[1,6,512]{2,1,0:T(8,128)(2,1)S(1)} %fusion.8), channel_id=1, replica_groups=mesh['grp'=8,'dev'=64] {'dev'}, dimensions={0}, use_global_device_ids=true | all-gather | bytes 399360 | tf_op jit(solution)/shard_map/all_gather | solution.py:26
  146.8 0.1 reshape.96
  147.0 0.9 fusion
  147.9 0.0 all-gather.6.cloned.1.call-update
  147.9 0.1 copy.24
  148.0 0.1 min.12
  148.1 0.1 copy.22
  148.2 0.1 copy.23
  148.3 0.1 copy.25
  148.4 112.1 %all-gather.6.cloned.1.call-done = bf16[8192,512]{1,0:T(8,128)(2,1)} async-done(((bf16[128,512]{1,0:T(8,128)(2,1)}), bf16[8192,512]{1,0:T(8,128)(2,1)}) %all-gather.6.cloned.1.call-update) | async-done | bytes 8388624 | tf_op jit(solution)/shard_map/all_gather | solution.py:39
  260.5 5.7 %gather_fusion = bf16[256,512]{1,0:T(8,128)(2,1)S(1)} fusion(bf16[8192,512]{1,0:T(8,128)(2,1)} %all-gather.6.cloned.1.call-done, s32[1024]{0:T(1024)S(1)} %pad_clamp_fusion), kind=kCustom, calls=%fused_computation | custom fusion | bytes 525312 | tf_op jit(solution)/shard_map/jit(_take)/gather | solution.py:41
  266.2 0.1 fusion.4
  266.3 0.3 fusion.1
  266.6 0.3 fusion.3
  266.9 0.1 copy.27
  267.0 0.1 copy.31
  267.1 22.7 %all-reduce = (f32[32,9]{0,1:T(8,128)S(1)}, f32[32,9]{0,1:T(8,128)S(1)}) all-reduce(f32[32,9]{0,1:T(8,128)S(1)} %bitcast.28, f32[32,9]{0,1:T(8,128)S(1)} %copy.31), channel_id=1, replica_groups=mesh['grp'=8,'dev'=64] {'grp'}, use_global_device_ids=true, to_apply=%region_2.3 | all-reduce | flops 576 | bytes 4608 | tf_op jit(solution)/shard_map/psum | solution.py:53
  289.8 0.5 fusion.10
  290.4 0.1 multiply_bitcast_fusion
  290.4 0.1 copy.32
  290.5 0.4 fusion.2
  291.0 0.6 copy.38
  (15 shorter events, 0.1 us)
Async XLA Ops:
  7.2 259.4 %copy-start = (bf16[32,512]{1,0:T(8,128)(2,1)S(1)}, bf16[32,512]{1,0:T(8,128)(2,1)}, u32[]{:S(2)}) copy-start(bf16[32,512]{1,0:T(8,128)(2,1)} %param.14) | copy-start | bytes 98308
  7.2 92.7 %all-gather.4.cloned.1.call-start = ((), (), s32[]{:S(2)}) async-start(), calls=%async_computation | async-start | bytes 4259840 | tf_op jit(solution)/shard_map/all_gather | solution.py:21
  7.9 252.6 %all-gather.6.cloned.1.call-start = ((), (), s32[]{:S(2)}) async-start(), calls=%async_computation.1 | async-start | bytes 8519680 | tf_op jit(solution)/shard_map/all_gather | solution.py:39
  110.4 36.6 %copy-start.1 = (bf16[128,512]{1,0:T(8,128)(2,1)S(1)}, bf16[128,512]{1,0:T(8,128)(2,1)}, u32[]{:S(2)}) copy-start(bf16[128,512]{1,0:T(8,128)(2,1)} %param.10) | copy-start | bytes 393220
  110.4 37.5 %copy-start.3 = (s32[32,8]{0,1:T(8,128)S(1)}, s32[32,8]{0,1:T(8,128)}, u32[]{:S(2)}) copy-start(s32[32,8]{0,1:T(8,128)} %param.13) | copy-start | bytes 3076
  110.4 37.5 %copy-start.4 = (s32[32,8]{0,1:T(8,128)S(1)}, s32[32,8]{0,1:T(8,128)}, u32[]{:S(2)}) copy-start(s32[32,8]{0,1:T(8,128)} %param.12) | copy-start | bytes 3076
  110.4 37.9 %copy-start.2 = (bf16[32,512]{1,0:T(8,128)(2,1)S(1)}, bf16[32,512]{1,0:T(8,128)(2,1)}, u32[]{:S(2)}) copy-start(bf16[32,512]{1,0:T(8,128)(2,1)} %param.15) | copy-start | bytes 98308
Sparse Core Ops, SparseCore 0:
  11.1 88.7 all-gather.3
  148.0 112.4 all-gather.5
where the time goes:
time: 301 us; the launch traced here: 298 us
  waiting for transfers between devices  204 us (68%)
  blocking collectives  58.7 us (20%)
  between operations  14.2 us (5%)
  matrix products  12.2 us (4%)
  local copies, waits for them, and re-layouts  7.12 us (2%)
    all_gather x1, waiting for transfers between devices, body(): piece = lax.all_gather(new_bank, 'dev', axis=0, tiled=True)  112 us
    all_gather x1, waiting for transfers between devices, body(): lax.all_gather(ckpt_weight, 'dev', axis=0, tiled=True)  91.1 us
    all_gather x1, blocking collectives, body(): all_encoded = lax.all_gather(encoded, 'dev', axis=0, tiled=True)  36.1 us
    psum x1, blocking collectives, body(): dot_sums, square_sums = lax.psum((dot_sums, square_sums), 'grp')  22.7 us
    dot_general x1, matrix products, body(): jnp.dot(passages, lax.all_gather(ckpt_weight, 'dev', axis=0, tiled=True),...  10.5 us
  transfers between devices with their start and end apart: 2, of which 2 were waited for; matrix products, arithmetic and copies ran while one was open for 0% of the time, Pallas kernels for 0%

commit v1 on v0

v1 whole, which is shorter than its diff:
```python
import math

import jax
import jax.numpy as jnp
from jax import lax
from jax.experimental import pallas as pl
from jax.experimental.pallas import tpu as pltpu
from jax.sharding import PartitionSpec as P

MESH = pl.DeviceIdType.MESH
F32, BF16, I32 = jnp.float32, jnp.bfloat16, jnp.int32

D = 4096
PLEN = 256
SIDE = 8
GRP = 8
NEG = 8
CAP = 8
QD = 32
BANK = 128
COLS = 512
HALF = 256
DEPTH = 64
TOK = 1536
NPAS = TOK // PLEN
REQ = QD * NEG
SLOTS = SIDE * SIDE * CAP


def iota(shape, dim):
    return lax.broadcasted_iota(I32, shape, dim)


def wrap(v):
    return lax.rem(v + 2 * SIDE, SIDE)


def rel(j):
    return (1 - 2 * (j % 2)) * ((j + 1) // 2)


def dot(a, b):
    return jnp.dot(a, b, preferred_element_type=F32)


def ones(mask):
    return jnp.where(mask, 1.0, 0.0).astype(BF16)


def spread(x):
    left = x[:, :128].reshape(64, 8, 128)
    right = x[:, 128:].reshape(64, 8, 128)
    return jnp.concatenate([left, right], axis=1).astype(BF16)


def joined(x):
    x = x.astype(F32)
    left = x[:, :8].reshape(SLOTS, 128)
    right = x[:, 8:].reshape(SLOTS, 128)
    return jnp.concatenate([left, right], axis=1).astype(BF16)


def kernel(
    pas, w, bank, touched, owner, row, queries, positives,
    new_bank, losses, direction,
    pas_a, pas_b, w_a, w_b, acc,
    v_bank, v_touched, v_owner, v_row, v_q, v_pos, v_new, v_dir,
    t1, r1, r1t, r2, sb0, sb1, rb0, rb1, rr0, rr1, fr0, fr1,
    sel0, sel1, mat0, mat1, nb0, nb1, stats,
    s_in, s_pas, s_own, w1s, w1r, w2s, w2r, qs, qr, as_, ar, fs, frs, gs, gr, s_out,
):
    d = lax.axis_index("dev")
    g = lax.axis_index("grp")
    z, y = d // SIDE, lax.rem(d, SIDE)

    def at(dz, dy):
        return {"dev": wrap(z + dz) * SIDE + wrap(y + dy)}

    def along(axis, k):
        return at(k, 0) if axis == 0 else at(0, k)

    def remote(src, dst, send, recv, to):
        return pltpu.make_async_remote_copy(src, dst, send, recv, device_id=to, device_id_type=MESH)

    small = [
        (owner, v_owner), (row, v_row), (touched, v_touched), (bank, v_bank), (queries, v_q), (positives, v_pos)
    ]
    loads = [pltpu.make_async_copy(a, b, s_in.at[i]) for i, (a, b) in enumerate(small)]
    for c in loads:
        c.start()
    own_a = pltpu.make_async_copy(w.at[:, pl.ds(0, HALF)], w_a.at[y // 2, z, y % 2], s_own.at[0])
    own_b = pltpu.make_async_copy(w.at[:, pl.ds(HALF, HALF)], w_b.at[z, y], s_own.at[1])
    own_a.start()
    own_b.start()

    barrier = pltpu.get_barrier_semaphore()
    for k in range(1, SIDE):
        pl.semaphore_signal(barrier, inc=1, device_id=at(k, 0), device_id_type=MESH)
        pl.semaphore_signal(barrier, inc=1, device_id=at(0, k), device_id_type=MESH)
    for k in range(1, GRP):
        pl.semaphore_signal(barrier, inc=1, device_id={"grp": lax.rem(g + k, GRP)}, device_id_type=MESH)

    def load_b(k):
        zz = wrap(z + k)
        return pltpu.make_async_copy(pas.at[:, pl.ds(pl.multiple_of(zz * COLS, COLS), COLS)], pas_b.at[zz], s_pas.at[zz])

    for j in range(SIDE):
        load_b(rel(j)).start()
    flip = 2 * (y % 2) - 1
    pairs = [lax.rem(y // 2 + k + 8, 4) for k in (0, flip, -flip, 2)]
    for m in pairs:
        for zz in range(SIDE):
            pltpu.make_async_copy(
                pas.at[:, pl.ds(pl.multiple_of(zz * COLS + m * 128, 128), 128)],
                pas_a.at[m, :, pl.ds(zz * 128, 128)],
                s_pas.at[SIDE + m],
            ).start()

    pl.semaphore_wait(barrier, 2 * (SIDE - 1) + GRP - 1)

    def block(h, zz, yy):
        return w_a.at[yy // 2, zz, lax.rem(yy, 2)] if h == 0 else w_b.at[zz, yy]

    def mine(h):
        return w.at[:, pl.ds(h * HALF, HALF)]

    def name(h, j, k):
        return block(h, wrap(z + j), wrap(y + k)) if h == 0 else block(h, wrap(z + k), wrap(y + j))

    ORDER1 = (1, -1, 2, -2, 3, -3, 4)

    def first(h, src, came, delta):
        i = h * 7 + ORDER1.index(came + delta)
        b = name(h, -came, 0)
        return remote(b if src is None else src, b, w1s.at[i], w1r.at[i], along(h, delta))

    def second(h, way, s, j):
        i = (h * 2 + (1 - way) // 2) * 4 + s - 1
        b = name(h, rel(j), -way * (s - 1))
        src = mine(h) if s == 1 and isinstance(j, int) and j == 0 else b
        return remote(src, b, w2s.at[i], w2r.at[i, j], along(1 - h, way))

    firsts = []

    def go(c):
        c.start()
        firsts.append(c)

    for delta in (1, -1):
        for h in range(2):
            go(first(h, mine(h), 0, delta))
    for h in range(2):
        for way in (1, -1):
            second(h, way, 1, 0).start()
    for delta in (2, -2):
        for h in range(2):
            go(first(h, mine(h), 0, delta))

    def got_first(h, came):
        i = h * 7 + ORDER1.index(came)
        b = name(h, -came, 0)
        remote(b, b, w1s.at[i], w1r.at[i], along(h, 1)).wait_recv()

    place = {1: 1, -1: 2, 2: 3, -2: 4, 3: 5, -3: 6, 4: 7}

    for c in loads[:2]:
        c.wait()
    own_col = jnp.concatenate([v_owner[:, j : j + 1] for j in range(NEG)], axis=0)
    row_col = jnp.concatenate([v_row[:, j : j + 1] for j in range(NEG)], axis=0)
    own_zy = own_col
    own_yz = lax.rem(own_col, SIDE) * SIDE + own_col // SIDE
    named = ones(own_yz == iota((REQ, 128), 1))
    before = dot(ones(iota((REQ, REQ), 0) > iota((REQ, REQ), 1)), named)
    rank = jnp.sum(named.astype(F32) * before, axis=1, keepdims=True).astype(I32)
    entry = jnp.where(rank == iota((REQ, 128), 1), (row_col + 1).astype(F32), 0.0).astype(BF16)
    table = lax.dot_general(named, entry, (((0,), (0,)), ((), ())), preferred_element_type=F32)
    t1[...] = table[: SIDE * SIDE].reshape(SIDE, SIDE, 128)
    r1[pl.ds(y, 1)] = t1[pl.ds(y, 1)]

    def ask1(k):
        return remote(t1.at[wrap(y + k)], r1.at[y], qs.at[k - 1], qr.at[k - 1], at(0, k))

    def ask2(k):
        return remote(r1t.at[wrap(z + k)], r2.at[z], qs.at[6 + k], qr.at[6 + k], at(k, 0))

    for k in range(1, SIDE):
        ask1(k).start()

    for came in (1, -1):
        for h in range(2):
            got_first(h, came)
            for way in (1, -1):
                second(h, way, 1, place[came]).start()
    for came in (2, -2):
        for h in range(2):
            got_first(h, came)
            go(first(h, None, came, 1 if came > 0 else -1))
            if came > 0:
                go(first(h, None, came, 2))
            for way in (1, -1):
                second(h, way, 1, place[came]).start()

    for c in loads[2:4]:
        c.wait()
    p384, q512 = iota((NPAS * 64, SLOTS), 0), iota((NPAS * 64, SLOTS), 1)
    blk, i_ = q512 // 8, lax.rem(q512, 8)
    ids = v_touched[...]
    hilo = jnp.concatenate(
        [(ids // BANK + 1).astype(F32), lax.rem(ids, BANK).astype(F32), jnp.zeros((6, NPAS * 64), F32)], axis=0
    ).astype(BF16)

    def masks(h, own_pos, sel, mat, nb):
        dev_of = blk if h == 0 else lax.rem(blk, SIDE) * SIDE + blk // SIDE
        perm = ones((dev_of * NPAS + i_ == p384) & (i_ < NPAS))
        where = dot(hilo, perm)
        hi, lo = where[0:1].astype(I32), where[1:2].astype(I32)
        hit = (own_col + 1 == hi) & (row_col == lo)
        mat[...] = ones(hit)
        some = jnp.sum(jnp.where(hit, 1.0, 0.0), axis=1, keepdims=True)
        slot = own_pos * CAP + rank
        sel[...] = ones((slot == iota((REQ, SLOTS), 1)) & (some < 0.5))
        nb[...] = ones((hi == d + 1) & (lo == iota((BANK, SLOTS), 0)))

    masks(0, own_zy, sel0, mat0, nb0)

    for k in range(1, SIDE):
        ask1(k).wait_recv()
    zy = iota((64, 64), 0)
    swap = ones(lax.rem(zy, SIDE) * SIDE + zy // SIDE == iota((64, 64), 1))
    r1t[...] = dot(swap, r1[...].reshape(64, 128).astype(BF16)).reshape(SIDE, SIDE, 128)
    r2[pl.ds(z, 1)] = r1t[pl.ds(z, 1)]
    for k in range(1, SIDE):
        ask2(k).start()

    for came in (3, -3, 4):
        for h in range(2):
            got_first(h, came)
            for way in (1, -1):
                second(h, way, 1, place[came]).start()

    masks(1, own_yz, sel1, mat1, nb1)
    own_a.wait()
    own_b.wait()

    for k in range(1, SIDE):
        ask2(k).wait_recv()

    def answer(h, sb):
        p, r = iota((SLOTS, 64), 0) // 8, iota((SLOTS, 64), 1)
        asker = lax.rem(p, SIDE) * SIDE + p // SIDE if h == 0 else p
        lines = dot(ones(asker == r), r2[...].reshape(64, 128).astype(BF16))
        own = lax.rem(iota((SLOTS, 128), 0), 8) == iota((SLOTS, 128), 1)
        want = jnp.sum(jnp.where(own, lines, 0.0), axis=1, keepdims=True).astype(I32)
        pick = ones(want == iota((SLOTS, BANK), 1) + 1)
        out = dot(pick, v_bank[:, h * HALF : (h + 1) * HALF])
        sb[...] = spread(out).reshape(SIDE, SIDE, 16, 128)

    answer(0, sb0)
    answer(1, sb1)
    rb0[pl.ds(y, 1)] = sb0[pl.ds(y, 1)]
    rb1[pl.ds(z, 1)] = sb1[pl.ds(z, 1)]

    def rows1(h, k):
        i = h * 7 + k - 1
        if h == 0:
            return remote(sb0.at[wrap(y + k)], rb0.at[y], as_.at[i], ar.at[i], at(0, k))
        return remote(sb1.at[wrap(z + k)], rb1.at[z], as_.at[i], ar.at[i], at(k, 0))

    def rows2(h, k):
        i = 14 + h * 7 + k - 1
        if h == 0:
            return remote(rb0.at[:, wrap(z + k)], rr0.at[z], as_.at[i], ar.at[i], at(k, 0))
        return remote(rb1.at[:, wrap(y + k)], rr1.at[y], as_.at[i], ar.at[i], at(0, k))

    PIECE = TOK // 4

    def loaded_b(k):
        load_b(k).wait()

    def loaded_a(m):
        pltpu.make_async_copy(pas_a.at[m], pas_a.at[m], s_pas.at[SIDE + m]).wait()

    def unit_a(m, rows):
        return dot(pas_a[m, rows, :], w_a[m].reshape(1024, HALF))

    def unit_b(k, rows):
        zz = wrap(z + k)
        return dot(pas_b[zz, rows, :], w_b[zz].reshape(COLS, HALF))

    def arrived(s, j):
        for h in range(2):
            for way in (1, -1):
                second(h, way, s, j).wait_recv()

    def forwards(s, j, ways):
        for h in range(2):
            for way in ways:
                second(h, way, s, j).start()

    def received(s, j, ways):
        i0 = s - 1
        for h in range(2):
            for way in (1, -1):
                i = (h * 2 + (1 - way) // 2) * 4 + i0
                b = name(h, rel(j), -way * s)
                if s < 4 or way in ways:
                    remote(b, b, w2s.at[i], w2r.at[i, j], along(1 - h, way)).wait_recv()
                    if way in ways and s < 4:
                        second(h, way, s + 1, j).start()

    def ring_step(s, compute_a, compute_b):
        def turn(t, ways):
            rows = pl.ds(pl.multiple_of(t * PIECE, PIECE), PIECE)
            received(s, 2 * t, ways)
            if compute_a is not None:
                compute_a(rows)
            received(s, 2 * t + 1, ways)
            if compute_b is not None:
                compute_b(rows)

        def loop(lo, hi, ways):
            lax.fori_loop(lo, hi, lambda t, c: (turn(t, ways), c)[1], 0)

        if s < 3:
            loop(0, 4, (1, -1))
        else:
            loop(0, 2, (1,))
            loop(2, 4, (-1,))

    left, right = pl.ds(0, HALF), pl.ds(HALF, HALF)

    def first_b(rows):
        acc[rows, right] = unit_b(0, rows)

    def first_a(rows):
        acc[rows, left] = unit_a(pairs[0], rows)

    def more_a(k):
        def run(rows):
            acc[rows, left] += unit_a(pairs[k], rows)

        return run

    def more_b(s):
        def run(rows):
            acc[rows, right] += unit_b(s, rows) + unit_b(-s, rows)

        return run

    loaded_b(0)
    ring_step(1, None, first_b)
    loaded_b(1)
    loaded_b(-1)
    loaded_a(pairs[0])
    ring_step(2, first_a, more_b(1))
    loaded_b(2)
    loaded_b(-2)
    loaded_a(pairs[1])
    ring_step(3, more_a(1), more_b(2))
    for h in range(2):
        for k in range(1, SIDE):
            rows1(h, k).start()
    loaded_b(3)
    loaded_b(-3)
    loaded_a(pairs[2])
    ring_step(4, more_a(2), more_b(3))
    loaded_b(4)
    loaded_a(pairs[3])

    enc_a, enc_b = [], []
    for i in range(NPAS):
        rows = pl.ds(i * PLEN, PLEN)
        enc_a.append(jnp.sum(jnp.tanh(acc[rows, left] + unit_a(pairs[3], rows)), axis=0, keepdims=True))
        enc_b.append(jnp.sum(jnp.tanh(acc[rows, right] + unit_b(4, rows)), axis=0, keepdims=True))

    def tile(enc):
        e = jnp.concatenate(enc + [jnp.zeros((2, HALF), F32)], axis=0) / math.sqrt(PLEN)
        return jnp.concatenate([e[:, :128], e[:, 128:]], axis=0).astype(BF16).reshape(1, 1, 16, 128)

    fr0[pl.ds(z, 1), pl.ds(y, 1)] = tile(enc_a)
    fr1[pl.ds(y, 1), pl.ds(z, 1)] = tile(enc_b)

    def fresh1(h, k):
        i = h * 7 + k - 1
        if h == 0:
            return remote(fr0.at[z, y], fr0.at[z, y], fs.at[i], frs.at[i], at(0, k))
        return remote(fr1.at[y, z], fr1.at[y, z], fs.at[i], frs.at[i], at(k, 0))

    def fresh2(h, k):
        i = 14 + h * 7 + k - 1
        if h == 0:
            return remote(fr0.at[z], fr0.at[z], fs.at[i], frs.at[i], at(k, 0))
        return remote(fr1.at[y], fr1.at[y], fs.at[i], frs.at[i], at(0, k))

    def each(make, what):
        for k in range(1, SIDE):
            for h in range(2):
                getattr(make(h, k), what)()

    each(fresh1, "start")
    each(rows1, "wait_recv")
    each(rows2, "start")
    rr0[pl.ds(z, 1)] = rb0[:, pl.ds(z, 1)].reshape(1, SIDE, 16, 128)
    rr1[pl.ds(y, 1)] = rb1[:, pl.ds(y, 1)].reshape(1, SIDE, 16, 128)
    each(fresh1, "wait_recv")
    each(fresh2, "start")
    each(fresh2, "wait_recv")

    outs = []
    fresh = []
    for h, (fr, nb) in enumerate(((fr0, nb0), (fr1, nb1))):
        rows_h = joined(fr[...].reshape(64, 16, 128))
        fresh.append(rows_h)
        hit = nb[...]
        some = jnp.sum(hit.astype(F32), axis=1, keepdims=True)
        cols = slice(h * HALF, (h + 1) * HALF)
        placed = jnp.where(some > 0.5, dot(hit, rows_h), v_bank[:, cols].astype(F32))
        v_new[:, cols] = placed.astype(BF16)
    outs.append(pltpu.make_async_copy(v_new, new_bank, s_out.at[0]))
    outs[0].start()
    patched = [dot(m[...], f) for m, f in zip((mat0, mat1), fresh, strict=True)]
    loads[4].wait()
    loads[5].wait()

    each(rows2, "wait_recv")
    negs = [
        dot(s[...], joined(r[...].reshape(64, 16, 128))) + p
        for s, r, p in zip((sel0, sel1), (rr0, rr1), patched, strict=True)
    ]
    keys = [v_pos[...].astype(F32)]
    for j in range(NEG):
        keys.append(jnp.concatenate([n[j * QD : (j + 1) * QD] for n in negs], axis=1))
    q = v_q[...].astype(F32)
    lane = iota((QD, 128), 1)
    st = jnp.zeros((QD, 128), F32)
    for k, key in enumerate(keys):
        st = jnp.where(lane == k, jnp.sum(q * key, axis=1, keepdims=True), st)
        st = jnp.where(lane == 64 + k, jnp.sum(key * key, axis=1, keepdims=True), st)
    stats[pl.ds(g, 1)] = st.reshape(1, QD, 128)

    def share(k):
        return remote(stats.at[g], stats.at[g], gs.at[k - 1], gr.at[k - 1], {"grp": lax.rem(g + k, GRP)})

    for k in range(1, GRP):
        share(k).start()
    for k in range(1, GRP):
        share(k).wait_recv()
    total = stats[0]
    for k in range(1, GRP):
        total = total + stats[k]
    dots = total[:, :64]
    squares = total[:, 64:]
    valid = iota((QD, 64), 1) < NEG + 1
    inverse = lax.rsqrt(squares / D + 1e-06)
    scores = dots * inverse / math.sqrt(D)
    highest = jnp.max(jnp.where(valid, scores, -jnp.inf), axis=1, keepdims=True)
    weights = jnp.where(valid, jnp.exp(scores - highest), 0.0)
    summed = jnp.sum(weights, axis=1, keepdims=True)
    loss = highest + jnp.log(summed) - scores[:, 0:1]
    target = jnp.where(iota((QD, 64), 1) == 0, 1.0, 0.0)
    coefficient = (weights / summed - target) * inverse
    grad = coefficient[:, 0:1] * keys[0]
    for k in range(1, NEG + 1):
        grad = grad + coefficient[:, k : k + 1] * keys[k]
    v_dir[...] = grad
    outs.append(pltpu.make_async_copy(v_dir, direction, s_out.at[1]))
    outs[1].start()
    eye = iota((QD, QD), 0) == iota((QD, QD), 1)
    losses[...] = jnp.sum(jnp.where(eye, loss, 0.0), axis=0, keepdims=True)

    for c in firsts:
        c.wait_send()
    for h in range(2):
        for way in range(2):
            for s in range(1, 5):
                sent = w_b.at[0] if s < 4 else w_b.at[0, pl.ds(0, 4)]
                pltpu.make_async_copy(sent, sent, w2s.at[(h * 2 + way) * 4 + s - 1]).wait()
    for k in range(1, SIDE):
        ask1(k).wait_send()
        ask2(k).wait_send()
    for make in (rows1, rows2, fresh1, fresh2):
        each(make, "wait_send")
    for k in range(1, GRP):
        share(k).wait_send()
    for c in outs:
        c.wait()


def body(passages, ckpt_weight, old_bank, touched, neg_owner, neg_row, queries, positives):
    anywhere = pl.BlockSpec(memory_space=pl.ANY)
    vmem = pl.BlockSpec(memory_space=pltpu.VMEM)
    dma = pltpu.SemaphoreType.DMA
    V = pltpu.VMEM
    slots = V((SIDE, SIDE, 16, 128), BF16)
    new_bank, losses, direction = pl.pallas_call(
        kernel,
        out_shape=(
            jax.ShapeDtypeStruct((BANK, COLS), BF16),
            jax.ShapeDtypeStruct((1, QD), F32),
            jax.ShapeDtypeStruct((QD, COLS), F32),
        ),
        in_specs=[anywhere] * 8,
        out_specs=(anywhere, vmem, anywhere),
        scratch_shapes=[
            V((4, TOK, 1024), BF16),
            V((SIDE, TOK, COLS), BF16),
            V((4, SIDE, 2, DEPTH, HALF), BF16),
            V((SIDE, SIDE, DEPTH, HALF), BF16),
            V((TOK, COLS), F32),
            V((BANK, COLS), BF16),
            V((1, NPAS * 64), I32),
            V((QD, NEG), I32),
            V((QD, NEG), I32),
            V((QD, COLS), BF16),
            V((QD, COLS), BF16),
            V((BANK, COLS), BF16),
            V((QD, COLS), F32),
            *[V((SIDE, SIDE, 128), F32)] * 4,
            *[slots] * 8,
            *[V((REQ, SLOTS), BF16)] * 4,
            *[V((BANK, SLOTS), BF16)] * 2,
            V((GRP, QD, 128), F32),
            dma((6,)),
            dma((12,)),
            dma((2,)),
            dma((14,)),
            dma((14,)),
            dma((16,)),
            dma((16, 8)),
            dma((14,)),
            dma((14,)),
            dma((28,)),
            dma((28,)),
            dma((28,)),
            dma((28,)),
            dma((7,)),
            dma((7,)),
            dma((2,)),
        ],
        compiler_params=pltpu.CompilerParams(
            collective_id=0, has_side_effects=True, vmem_limit_bytes=60 * 1024 * 1024
        ),
    )(passages, ckpt_weight, old_bank, touched.reshape(1, -1), neg_owner, neg_row, queries, positives)
    return new_bank, losses.reshape(-1), direction


def solution(mesh):
    return jax.shard_map(
        body,
        mesh=mesh,
        in_specs=(
            P("dev", None),
            P("dev", "grp"),
            P("dev", "grp"),
            P(),
            P("dev", None),
            P("dev", None),
            P("dev", "grp"),
            P("dev", "grp"),
        ),
        out_specs=(P("dev", "grp"), P("dev"), P("dev", "grp")),
        check_vma=False,
    )
```

time: 301 us -> 82.3 us (0.27)
  waiting for transfers between devices: 204 us -> 0 us
  Pallas kernels: 0 us -> 73.2 us
  blocking collectives: 58.7 us -> 0 us
  between operations: 14.2 us -> 0.64 us
  matrix products: 12.2 us -> 0 us
    all_gather x2 -> x0, waiting for transfers between devices: 203 us -> none  [the longest x1 112 us: body(): piece = lax.all_gather(new_bank, 'dev', axis=0, tiled=True)]
    pallas_call x0 -> x1, Pallas kernels: none -> 73.2 us  [body(): pl.pallas_call(kernel, out_shape=(jax.ShapeDtypeStruct((BANK, COLS), BF16...]
    all_gather x1 -> x0, blocking collectives: 36.1 us -> none  [body(): all_encoded = lax.all_gather(encoded, 'dev', axis=0, tiled=True)]
    psum x1 -> x0, blocking collectives: 22.7 us -> none  [body(): dot_sums, square_sums = lax.psum((dot_sums, square_sums), 'grp')]
    dot_general x4 -> x0, matrix products: 12.2 us -> none  [the longest x1 10.5 us: body(): jnp.dot(passages, lax.all_gather(ckpt_weight, 'dev', axis=0, tiled=True),...]
    unnamed x11 -> x5, local copies, waits for them, and re-layouts: 0.17 us -> 6.89 us
    gather x1 -> x0, local copies, waits for them, and re-layouts: 5.67 us -> none  [body(): jnp.take(piece, jnp.clip(global_ids, 0, piece.shape[0] - 1), axis=0)]
  transfers between devices with their start and end apart: 2 -> 0, of which waited for: 2 -> 0; matrix products, arithmetic and copies ran while one was open for 0% -> 0% of each run, Pallas kernels for 0% -> 0%
where the time goes in v1:
time: 82.3 us; the launch traced here: 82 us
  Pallas kernels  73.2 us (89%)
  local copies, waits for them, and re-layouts  8.13 us (10%)
    pallas_call x1, Pallas kernels, body(): pl.pallas_call(kernel, out_shape=(jax.ShapeDtypeStruct((BANK, COLS), BF16...  73.2 us
    unnamed x5, local copies, waits for them, and re-layouts  6.89 us

profile of v1, /device:TPU:1, one launch (start us, length us, event | category | flops | bytes accessed | tf_op | source)
XLA Modules:
  0.0 82.0 jit_solution(7571435451495354316)
XLA Ops:
  0.6 1.2 %reshape.12.touched = s32[1,384]{1,0:T(1,128)} reshape(s32[384]{0:T(512)} %param.11) | data formatting | bytes 3072 | tf_op jit(solution)/shard_map/reshape | solution.py:543
  1.9 1.4 %copy.11.owner = s32[32,8]{1,0:T(8,128)} copy(s32[32,8]{0,1:T(8,128)} %param.12) | data formatting | bytes 2048 | tf_op args[4]
  3.2 1.4 %copy.12.row = s32[32,8]{1,0:T(8,128)} copy(s32[32,8]{0,1:T(8,128)} %param.13) | data formatting | bytes 2048 | tf_op args[5]
  4.6 73.2 %shard_map.103 = (bf16[128,512]{1,0:T(8,128)(2,1)}, f32[1,32]{1,0:T(1,128)}, f32[32,512]{1,0:T(8,128)}) custom-call(bf16[1536,4096]{1,0:T(8,128)(2,1)} %pas.1, bf16[64,512]{1,0:T(8,128)(2,1)} %w.1, bf16[128,512]{1,0:T(8,128)(2,1)} %bank.1, s32[1,384]{1,0:T(1,128)} %reshape.12.touched, s32[32,8]{1,0:T(8,128)} %copy.11.owner, s32[32,8]{1,0:T(8,128)} %copy.12.row, ...), custom_call_target="tpu_custom_call" | custom-call | tf_op jit(solution)/shard_map/pallas_call | solution.py:495
  77.8 1.6 %copy.16 = bf16[128,512]{1,0:T(8,128)(2,1)} copy(bf16[128,512]{1,0:T(8,128)(2,1)} %get-tuple-element.12) | data formatting | bytes 262144
  79.4 1.1 %copy.17 = f32[32]{0:T(128)} copy(f32[32]{0:T(128)} %bitcast.1) | data formatting | bytes 256
  80.5 1.5 %copy.18 = f32[32,512]{1,0:T(8,128)} copy(f32[32,512]{1,0:T(8,128)} %get-tuple-element.14) | data formatting | bytes 131072

commit v2 on v1

v2 whole, which is shorter than its diff:
```python
import math

import jax
import jax.numpy as jnp
from jax import lax
from jax.experimental import pallas as pl
from jax.experimental.pallas import tpu as pltpu
from jax.sharding import PartitionSpec as P

MESH = pl.DeviceIdType.MESH
F32, BF16, I32 = jnp.float32, jnp.bfloat16, jnp.int32

D = 4096
PLEN = 256
SIDE = 8
GRP = 8
NEG = 8
CAP = 8
QD = 32
BANK = 128
COLS = 512
HALF = 256
DEPTH = 64
TOK = 1536
NPAS = TOK // PLEN
REQ = QD * NEG
SLOTS = SIDE * SIDE * CAP


def iota(shape, dim):
    return lax.broadcasted_iota(I32, shape, dim)


def wrap(v):
    return lax.rem(v + 2 * SIDE, SIDE)


def rel(j):
    return (1 - 2 * (j % 2)) * ((j + 1) // 2)


def dot(a, b):
    return jnp.dot(a, b, preferred_element_type=F32)


def ones(mask):
    return jnp.where(mask, 1.0, 0.0).astype(BF16)


def spread(x):
    left = x[:, :128].reshape(64, 8, 128)
    right = x[:, 128:].reshape(64, 8, 128)
    return jnp.concatenate([left, right], axis=1).astype(BF16)


def joined(x):
    x = x.astype(F32)
    left = x[:, :8].reshape(-1, 128)
    right = x[:, 8:].reshape(-1, 128)
    return jnp.concatenate([left, right], axis=1).astype(BF16)


def kernel(
    pas, w, bank, touched, owner, row, queries, positives,
    new_bank, losses, direction,
    pas_a, pas_b, w_a, w_b, acc,
    v_bank, v_touched, v_owner, v_row, v_q, v_pos, v_new, v_dir,
    t1, r1, r1t, r2, sb0, sb1, rb0, rb1, rr0, rr1, fr0, fr1, fl0, fl1,
    sel0, sel1, mat0, mat1, nb0, nb1, stats,
    s_in, s_pas, s_own, w1s, w1r, w2s, w2r, qs, qr, as_, ar, fs, frs, gs, gr, s_out,
):
    d = lax.axis_index("dev")
    g = lax.axis_index("grp")
    z, y = d // SIDE, lax.rem(d, SIDE)

    def at(dz, dy):
        return {"dev": wrap(z + dz) * SIDE + wrap(y + dy)}

    def along(axis, k):
        return at(k, 0) if axis == 0 else at(0, k)

    def remote(src, dst, send, recv, to):
        return pltpu.make_async_remote_copy(src, dst, send, recv, device_id=to, device_id_type=MESH)

    small = [
        (owner, v_owner), (row, v_row), (touched, v_touched), (bank, v_bank), (queries, v_q), (positives, v_pos)
    ]
    loads = [pltpu.make_async_copy(a, b, s_in.at[i]) for i, (a, b) in enumerate(small)]
    for c in loads:
        c.start()
    own_a = pltpu.make_async_copy(w.at[:, pl.ds(0, HALF)], w_a.at[y // 2, z, y % 2], s_own.at[0])
    own_b = pltpu.make_async_copy(w.at[:, pl.ds(HALF, HALF)], w_b.at[z, y], s_own.at[1])
    own_a.start()
    own_b.start()

    barrier = pltpu.get_barrier_semaphore()
    for k in range(1, SIDE):
        pl.semaphore_signal(barrier, inc=1, device_id=at(k, 0), device_id_type=MESH)
        pl.semaphore_signal(barrier, inc=1, device_id=at(0, k), device_id_type=MESH)
    for k in range(1, GRP):
        pl.semaphore_signal(barrier, inc=1, device_id={"grp": lax.rem(g + k, GRP)}, device_id_type=MESH)

    def load_b(k):
        zz = wrap(z + k)
        return pltpu.make_async_copy(pas.at[:, pl.ds(pl.multiple_of(zz * COLS, COLS), COLS)], pas_b.at[zz], s_pas.at[zz])

    for j in range(SIDE):
        load_b(rel(j)).start()
    flip = 2 * (y % 2) - 1
    pairs = [lax.rem(y // 2 + k + 8, 4) for k in (0, flip, -flip, 2)]
    for m in pairs:
        for zz in range(SIDE):
            pltpu.make_async_copy(
                pas.at[:, pl.ds(pl.multiple_of(zz * COLS + m * 128, 128), 128)],
                pas_a.at[m, :, pl.ds(zz * 128, 128)],
                s_pas.at[SIDE + m],
            ).start()

    acc[:, :HALF] = jnp.zeros((TOK, HALF), F32)

    for c in loads[:2]:
        c.wait()
    eye = iota((QD, QD), 0) == iota((QD, QD), 1)

    def column(v):
        lines = v[...].astype(F32)
        parts = [jnp.sum(jnp.where(eye, lines[j : j + 1], 0.0), axis=1, keepdims=True) for j in range(NEG)]
        return jnp.concatenate(parts, axis=0).astype(I32)

    own_col, row_col = column(v_owner), column(v_row)
    own_zy = own_col
    own_yz = lax.rem(own_col, SIDE) * SIDE + own_col // SIDE
    named = ones(own_yz == iota((REQ, 128), 1))
    before = dot(ones(iota((REQ, REQ), 0) > iota((REQ, REQ), 1)), named)
    rank = jnp.sum(named.astype(F32) * before, axis=1, keepdims=True).astype(I32)
    entry = jnp.where(rank == iota((REQ, 128), 1), (row_col + 1).astype(F32), 0.0).astype(BF16)
    table = lax.dot_general(named, entry, (((0,), (0,)), ((), ())), preferred_element_type=F32)
    t1[...] = table[: SIDE * SIDE].reshape(SIDE, SIDE, 128)
    pl.semaphore_wait(barrier, 2 * (SIDE - 1) + GRP - 1)

    def block(h, zz, yy):
        return w_a.at[yy // 2, zz, lax.rem(yy, 2)] if h == 0 else w_b.at[zz, yy]

    def mine(h):
        return w.at[:, pl.ds(h * HALF, HALF)]

    def name(h, j, k):
        return block(h, wrap(z + j), wrap(y + k)) if h == 0 else block(h, wrap(z + k), wrap(y + j))

    ORDER1 = (1, -1, 2, -2, 3, -3, 4)

    def first(h, src, came, delta):
        i = h * 7 + ORDER1.index(came + delta)
        b = name(h, -came, 0)
        return remote(b if src is None else src, b, w1s.at[i], w1r.at[i], along(h, delta))

    def second(h, way, s, j):
        i = (h * 2 + (1 - way) // 2) * 4 + s - 1
        b = name(h, rel(j), -way * (s - 1))
        src = mine(h) if s == 1 and isinstance(j, int) and j == 0 else b
        return remote(src, b, w2s.at[i], w2r.at[i, j], along(1 - h, way))

    firsts = []

    def go(c):
        c.start()
        firsts.append(c)

    for delta in (1, -1):
        for h in range(2):
            go(first(h, mine(h), 0, delta))
    for h in range(2):
        for way in (1, -1):
            second(h, way, 1, 0).start()
    for delta in (2, -2):
        for h in range(2):
            go(first(h, mine(h), 0, delta))

    def got_first(h, came):
        i = h * 7 + ORDER1.index(came)
        b = name(h, -came, 0)
        remote(b, b, w1s.at[i], w1r.at[i], along(h, 1)).wait_recv()

    place = {1: 1, -1: 2, 2: 3, -2: 4, 3: 5, -3: 6, 4: 7}

    r1[pl.ds(y, 1)] = t1[pl.ds(y, 1)]

    def ask1(k):
        return remote(t1.at[wrap(y + k)], r1.at[y], qs.at[k - 1], qr.at[k - 1], at(0, k))

    def ask2(k):
        return remote(r1t.at[wrap(z + k)], r2.at[z], qs.at[6 + k], qr.at[6 + k], at(k, 0))

    for k in range(1, SIDE):
        ask1(k).start()

    for came in (1, -1):
        for h in range(2):
            got_first(h, came)
            for way in (1, -1):
                second(h, way, 1, place[came]).start()
    for came in (2, -2):
        for h in range(2):
            got_first(h, came)
            go(first(h, None, came, 1 if came > 0 else -1))
            if came > 0:
                go(first(h, None, came, 2))
            for way in (1, -1):
                second(h, way, 1, place[came]).start()

    for came in (3, -3, 4):
        for h in range(2):
            got_first(h, came)
            for way in (1, -1):
                second(h, way, 1, place[came]).start()

    def ask_on():
        for k in range(1, SIDE):
            ask1(k).wait_recv()
        zy = iota((64, 64), 0)
        swap = ones(lax.rem(zy, SIDE) * SIDE + zy // SIDE == iota((64, 64), 1))
        r1t[...] = dot(swap, r1[...].reshape(64, 128).astype(BF16)).reshape(SIDE, SIDE, 128)
        r2[pl.ds(z, 1)] = r1t[pl.ds(z, 1)]
        for k in range(1, SIDE):
            ask2(k).start()

    def masks(h, own_pos, sel, mat, nb):
        ids = v_touched[...].reshape(1, NPAS * 64)
        hi, lo = ids // BANK, lax.rem(ids, BANK)
        if h == 1:
            halves = jnp.concatenate([hi.astype(F32), lo.astype(F32), jnp.zeros((6, NPAS * 64), F32)], axis=0).astype(BF16)
            spot = iota((1, NPAS * 64), 1)
            line, within = spot // (SIDE * NPAS), lax.rem(spot, SIDE * NPAS)
            source = (within // NPAS * SIDE + line) * NPAS + lax.rem(within, NPAS)
            moved = dot(halves, ones(source == iota((NPAS * 64, NPAS * 64), 0)))
            hi, lo = moved[0:1].astype(I32), moved[1:2].astype(I32)
        hit = (own_col == hi) & (row_col == lo)
        mat[...] = ones(hit)
        some = jnp.sum(jnp.where(hit, 1.0, 0.0), axis=1, keepdims=True)
        slot = own_pos * CAP + rank
        sel[...] = ones((slot == iota((REQ, SLOTS), 1)) & (some < 0.5))
        nb[...] = ones((hi == d) & (lo == iota((BANK, NPAS * 64), 0)))

    def answer(h, sb):
        p = iota((SLOTS, 1), 0) // 8
        asker = lax.rem(p, SIDE) * SIDE + p // SIDE if h == 0 else p
        lines = dot(ones(asker == iota((SLOTS, 64), 1)), r2[...].reshape(64, 128).astype(BF16))
        own = lax.rem(iota((SLOTS, 128), 0), 8) == iota((SLOTS, 128), 1)
        want = jnp.sum(jnp.where(own, lines, 0.0), axis=1, keepdims=True).astype(I32)
        pick = ones(want == iota((SLOTS, BANK), 1) + 1)
        out = dot(pick, v_bank[:, h * HALF : (h + 1) * HALF])
        sb[...] = spread(out).reshape(SIDE, SIDE, 16, 128)

    def answer_0():
        for k in range(1, SIDE):
            ask2(k).wait_recv()
        answer(0, sb0)
        rb0[pl.ds(y, 1)] = sb0[pl.ds(y, 1)]

    def answer_1():
        answer(1, sb1)
        rb1[pl.ds(z, 1)] = sb1[pl.ds(z, 1)]

    def rows1(h, k):
        i = h * 7 + k - 1
        if h == 0:
            return remote(sb0.at[wrap(y + k)], rb0.at[y], as_.at[i], ar.at[i], at(0, k))
        return remote(sb1.at[wrap(z + k)], rb1.at[z], as_.at[i], ar.at[i], at(k, 0))

    def rows2(h, k):
        i = 14 + h * 7 + k - 1
        if h == 0:
            return remote(rb0.at[:, wrap(z + k)], rr0.at[z], as_.at[i], ar.at[i], at(k, 0))
        return remote(rb1.at[:, wrap(y + k)], rr1.at[y], as_.at[i], ar.at[i], at(0, k))

    def loaded_b(k):
        load_b(k).wait()

    def loaded_a(m):
        pltpu.make_async_copy(pas_a.at[m], pas_a.at[m], s_pas.at[SIDE + m]).wait()

    def piece_a(m, t, rows=slice(None)):
        return dot(
            pas_a[m, rows, pl.ds(pl.multiple_of(t * 256, 256), 256)], w_a[m, pl.ds(2 * t, 2)].reshape(256, HALF)
        )

    def piece_b(k, t, rows=slice(None)):
        zz = wrap(z + k)
        return dot(
            pas_b[zz, rows, pl.ds(pl.multiple_of(t * 256, 256), 256)], w_b[zz, pl.ds(4 * t, 4)].reshape(256, HALF)
        )

    def received(s, j, ways):
        for h in range(2):
            for way in (1, -1):
                i = (h * 2 + (1 - way) // 2) * 4 + s - 1
                b = name(h, rel(j), -way * s)
                if s < 4 or way in ways:
                    remote(b, b, w2s.at[i], w2r.at[i, j], along(1 - h, way)).wait_recv()
                    if way in ways and s < 4:
                        second(h, way, s + 1, j).start()

    left, right = pl.ds(0, HALF), pl.ds(HALF, HALF)

    def ring_step(s, k):
        def turn_a(j, c):
            received(s, j, (1, -1) if s < 3 else (1,))
            acc[:, left] += piece_a(pairs[k], j)
            return c

        def turn_b(j, c):
            received(s, j, (1, -1) if s < 3 else (-1,))
            acc[:, right] += piece_b((s - 1) * (1 - 2 * ((j - 4) // 2)), lax.rem(j, 2))
            return c

        lax.fori_loop(0, 4, turn_a, 0)
        lax.fori_loop(4, 8, turn_b, 0)

    for c in loads[2:4]:
        c.wait()
    between = {
        0: ask_on,
        1: lambda: masks(0, own_zy, sel0, mat0, nb0),
        3: lambda: masks(1, own_yz, sel1, mat1, nb1),
        5: answer_0,
        7: answer_1,
    }
    for j in range(SIDE):
        received(1, j, (1, -1))
        if j in between:
            between[j]()
    own_a.wait()
    own_b.wait()
    loaded_b(0)
    acc[:, right] = piece_b(0, 0) + piece_b(0, 1)
    loaded_b(1)
    loaded_b(-1)
    loaded_a(pairs[0])
    ring_step(2, 0)
    loaded_b(2)
    loaded_b(-2)
    loaded_a(pairs[1])
    ring_step(3, 1)
    for h in range(2):
        for k in range(1, SIDE):
            rows1(h, k).start()
    loaded_b(3)
    loaded_b(-3)
    loaded_a(pairs[2])
    ring_step(4, 2)
    loaded_b(4)
    loaded_a(pairs[3])

    enc_a, enc_b = [], []
    for i in range(NPAS):
        rows = pl.ds(i * PLEN, PLEN)
        last_a = acc[rows, left] + dot(pas_a[pairs[3], rows, :], w_a[pairs[3]].reshape(1024, HALF))
        enc_a.append(jnp.sum(jnp.tanh(last_a), axis=0, keepdims=True))
        zz = wrap(z + 4)
        last_b = acc[rows, right] + dot(pas_b[zz, rows, :], w_b[zz].reshape(COLS, HALF))
        enc_b.append(jnp.sum(jnp.tanh(last_b), axis=0, keepdims=True))

    def tile(enc):
        e = jnp.concatenate(enc + [jnp.zeros((2, HALF), F32)], axis=0) / math.sqrt(PLEN)
        return jnp.concatenate([e[:, :128], e[:, 128:]], axis=0).astype(BF16).reshape(1, 16, 128)

    fr0[pl.ds(y, 1)] = tile(enc_a)
    fr1[pl.ds(z, 1)] = tile(enc_b)

    def fresh1(h, k):
        i = h * 7 + k - 1
        if h == 0:
            return remote(fr0.at[y], fr0.at[y], fs.at[i], frs.at[i], at(0, k))
        return remote(fr1.at[z], fr1.at[z], fs.at[i], frs.at[i], at(k, 0))

    def fresh2(h, k):
        i = 14 + h * 7 + k - 1
        if h == 0:
            return remote(fl0.at[z], fl0.at[z], fs.at[i], frs.at[i], at(k, 0))
        return remote(fl1.at[y], fl1.at[y], fs.at[i], frs.at[i], at(0, k))

    def each(make, what):
        for k in range(1, SIDE):
            for h in range(2):
                getattr(make(h, k), what)()

    each(fresh1, "start")
    each(rows1, "wait_recv")
    each(rows2, "start")
    each(fresh1, "wait_recv")
    kept = iota((SIDE * NPAS, 1), 0)
    keep = ones(kept // NPAS * 8 + lax.rem(kept, NPAS) == iota((SIDE * NPAS, 64), 1))
    fl0[pl.ds(z, 1)] = dot(keep, joined(fr0[...])).astype(BF16).reshape(1, SIDE * NPAS, HALF)
    fl1[pl.ds(y, 1)] = dot(keep, joined(fr1[...])).astype(BF16).reshape(1, SIDE * NPAS, HALF)
    each(fresh2, "start")
    rr0[pl.ds(z, 1)] = rb0[:, pl.ds(z, 1)].reshape(1, SIDE, 16, 128)
    rr1[pl.ds(y, 1)] = rb1[:, pl.ds(y, 1)].reshape(1, SIDE, 16, 128)
    loads[4].wait()
    loads[5].wait()
    each(rows2, "wait_recv")
    old = [dot(m[...], joined(r[...].reshape(64, 16, 128))) for m, r in ((sel0, rr0), (sel1, rr1))]
    each(fresh2, "wait_recv")
    fresh = [f[...].reshape(NPAS * 64, HALF) for f in (fl0, fl1)]
    negs = [o + dot(m[...], f) for o, m, f in zip(old, (mat0, mat1), fresh, strict=True)]
    keys = [v_pos[...].astype(F32)]
    for j in range(NEG):
        keys.append(jnp.concatenate([n[j * QD : (j + 1) * QD] for n in negs], axis=1))
    q = v_q[...].astype(F32)
    lane = iota((QD, 128), 1)
    st = jnp.zeros((QD, 128), F32)
    for k, key in enumerate(keys):
        st = jnp.where(lane == k, jnp.sum(q * key, axis=1, keepdims=True), st)
        st = jnp.where(lane == 16 + k, jnp.sum(key * key, axis=1, keepdims=True), st)
    packed = st[0:8]
    for a in range(1, 4):
        packed = packed + pltpu.roll(st[8 * a : 8 * a + 8], 32 * a, 1)
    stats[pl.ds(g, 1)] = packed.reshape(1, 8, 128)

    def share(k):
        return remote(stats.at[g], stats.at[g], gs.at[k - 1], gr.at[k - 1], {"grp": lax.rem(g + k, GRP)})

    for k in range(1, GRP):
        share(k).start()

    for h, nb in enumerate((nb0, nb1)):
        hit = nb[...]
        some = jnp.sum(hit.astype(F32), axis=1, keepdims=True)
        cols = slice(h * HALF, (h + 1) * HALF)
        v_new[:, cols] = jnp.where(some > 0.5, dot(hit, fresh[h]), v_bank[:, cols].astype(F32)).astype(BF16)
    outs = [pltpu.make_async_copy(v_new, new_bank, s_out.at[0])]
    outs[0].start()

    for k in range(1, GRP):
        share(k).wait_recv()
    total = stats[0]
    for k in range(1, GRP):
        total = total + stats[k]
    dots = jnp.concatenate([total] + [pltpu.roll(total, 128 - 32 * a, 1) for a in range(1, 4)], axis=0)
    squares = pltpu.roll(dots, 112, 1)
    valid = lane < NEG + 1
    inverse = lax.rsqrt(squares / D + 1e-06)
    scores = dots * inverse / math.sqrt(D)
    highest = jnp.max(jnp.where(valid, scores, -jnp.inf), axis=1, keepdims=True)
    weights = jnp.where(valid, jnp.exp(scores - highest), 0.0)
    summed = jnp.sum(weights, axis=1, keepdims=True)
    loss = highest + jnp.log(summed) - scores[:, 0:1]
    target = jnp.where(lane == 0, 1.0, 0.0)
    coefficient = (weights / summed - target) * inverse
    grad = coefficient[:, 0:1] * keys[0]
    for k in range(1, NEG + 1):
        grad = grad + coefficient[:, k : k + 1] * keys[k]
    v_dir[...] = grad
    outs.append(pltpu.make_async_copy(v_dir, direction, s_out.at[1]))
    outs[1].start()
    losses[...] = jnp.sum(jnp.where(eye, loss, 0.0), axis=0, keepdims=True)

    for c in firsts:
        c.wait_send()
    for h in range(2):
        for way in range(2):
            for s in range(1, 5):
                sent = w_b.at[0] if s < 4 else w_b.at[0, pl.ds(0, 4)]
                pltpu.make_async_copy(sent, sent, w2s.at[(h * 2 + way) * 4 + s - 1]).wait()
    for k in range(1, SIDE):
        ask1(k).wait_send()
        ask2(k).wait_send()
    for make in (rows1, rows2, fresh1, fresh2):
        each(make, "wait_send")
    for k in range(1, GRP):
        share(k).wait_send()
    for c in outs:
        c.wait()


def place(a, b, c, a_out, b_out, c_out):
    a_out[...] = a[...]
    b_out[...] = b[...]
    c_out[...] = c[...]


def body(passages, ckpt_weight, old_bank, touched, neg_owner, neg_row, queries, positives):
    anywhere = pl.BlockSpec(memory_space=pl.ANY)
    vmem = pl.BlockSpec(memory_space=pltpu.VMEM)
    dma = pltpu.SemaphoreType.DMA
    V = pltpu.VMEM
    slots = V((SIDE, SIDE, 16, 128), BF16)
    new_bank, losses, direction = pl.pallas_call(
        kernel,
        out_shape=(
            jax.ShapeDtypeStruct((BANK, COLS), BF16),
            jax.ShapeDtypeStruct((1, QD), F32),
            jax.ShapeDtypeStruct((QD, COLS), F32),
        ),
        in_specs=[anywhere] * 8,
        out_specs=(anywhere, vmem, anywhere),
        scratch_shapes=[
            V((4, TOK, 1024), BF16),
            V((SIDE, TOK, COLS), BF16),
            V((4, SIDE, 2, DEPTH, HALF), BF16),
            V((SIDE, SIDE, DEPTH, HALF), BF16),
            V((TOK, COLS), F32),
            V((BANK, COLS), BF16),
            V((NPAS * 64,), I32),
            V((NEG, QD), I32),
            V((NEG, QD), I32),
            V((QD, COLS), BF16),
            V((QD, COLS), BF16),
            V((BANK, COLS), BF16),
            V((QD, COLS), F32),
            *[V((SIDE, SIDE, 128), F32)] * 4,
            *[slots] * 6,
            *[V((SIDE, 16, 128), BF16)] * 2,
            *[V((SIDE, SIDE * NPAS, HALF), BF16)] * 2,
            *[V((REQ, SLOTS), BF16)] * 2,
            *[V((REQ, NPAS * 64), BF16)] * 2,
            *[V((BANK, NPAS * 64), BF16)] * 2,
            V((GRP, 8, 128), F32),
            dma((6,)),
            dma((12,)),
            dma((2,)),
            dma((14,)),
            dma((14,)),
            dma((16,)),
            dma((16, 8)),
            dma((14,)),
            dma((14,)),
            dma((28,)),
            dma((28,)),
            dma((28,)),
            dma((28,)),
            dma((7,)),
            dma((7,)),
            dma((2,)),
        ],
        compiler_params=pltpu.CompilerParams(
            collective_id=0, has_side_effects=True, vmem_limit_bytes=60 * 1024 * 1024
        ),
    )(passages, ckpt_weight, old_bank, touched, neg_owner.T, neg_row.T, queries, positives)
    results = (new_bank, losses, direction)
    new_bank, losses, direction = pl.pallas_call(
        place,
        out_shape=tuple(jax.ShapeDtypeStruct(r.shape, r.dtype) for r in results),
        in_specs=[vmem] * 3,
        out_specs=(vmem,) * 3,
    )(*results)
    return new_bank, losses.reshape(-1), direction


def solution(mesh):
    return jax.shard_map(
        body,
        mesh=mesh,
        in_specs=(
            P("dev", None),
            P("dev", "grp"),
            P("dev", "grp"),
            P(),
            P("dev", None),
            P("dev", None),
            P("dev", "grp"),
            P("dev", "grp"),
        ),
        out_specs=(P("dev", "grp"), P("dev"), P("dev", "grp")),
        check_vma=False,
    )
```

time: 82.3 us -> 75 us (0.911)
  local copies, waits for them, and re-layouts: 8.13 us -> 0 us
  Pallas kernels: 73.2 us -> 74.2 us
    unnamed x5 -> x0, local copies, waits for them, and re-layouts: 6.89 us -> none
    pallas_call x0 -> x1, Pallas kernels: none -> 1.59 us  [body(): pl.pallas_call(place, out_shape=tuple((jax.ShapeDtypeStruct(r.shape, r.dt...]
    reshape x1 -> x0, local copies, waits for them, and re-layouts: 1.25 us -> none  [body(): touched.reshape(1, -1)]
where the time goes in v2:
time: 75 us; the launch traced here: 74.9 us
  Pallas kernels  74.2 us (99%)
    pallas_call x1, Pallas kernels, body(): pl.pallas_call(kernel, out_shape=(jax.ShapeDtypeStruct((BANK, COLS), BF16...  72.6 us
    pallas_call x1, Pallas kernels, body(): pl.pallas_call(place, out_shape=tuple((jax.ShapeDtypeStruct(r.shape, r.dt...  1.59 us

profile of v2, /device:TPU:1, one launch (start us, length us, event | category | flops | bytes accessed | tf_op | source)
XLA Modules:
  0.0 74.9 jit_solution(4050179654158764888)
XLA Ops:
  0.6 72.6 %shard_map.103 = (bf16[128,512]{1,0:T(8,128)(2,1)}, f32[1,32]{1,0:T(1,128)}, f32[32,512]{1,0:T(8,128)}) custom-call(bf16[1536,4096]{1,0:T(8,128)(2,1)} %pas.1, bf16[64,512]{1,0:T(8,128)(2,1)} %w.1, bf16[128,512]{1,0:T(8,128)(2,1)} %bank.1, s32[384]{0:T(512)} %touched.1, s32[8,32]{1,0:T(8,128)} %bitcast.3, s32[8,32]{1,0:T(8,128)} %bitcast.4, ...), custom_call_target="tpu_custom_call" | custom-call | tf_op jit(solution)/shard_map/pallas_call | solution.py:487
  73.3 1.6 %shard_map.104 = (bf16[128,512]{1,0:T(8,128)(2,1)}, f32[1,32]{1,0:T(1,128)}, f32[32,512]{1,0:T(8,128)}) custom-call(bf16[128,512]{1,0:T(8,128)(2,1)} %get-tuple-element.9.a, f32[1,32]{1,0:T(1,128)} %get-tuple-element.10.b, f32[32,512]{1,0:T(8,128)} %get-tuple-element.11.c), custom_call_target="tpu_custom_call" | custom-call | tf_op jit(solution)/shard_map/pallas_call | solution.py:540

commit v3 on v2

--- a/solution.py
+++ b/solution.py
@@ -48,8 +48,8 @@
 
 
 def spread(x):
-    left = x[:, :128].reshape(64, 8, 128)
-    right = x[:, 128:].reshape(64, 8, 128)
+    left = x[:, :128].reshape(-1, 8, 128)
+    right = x[:, 128:].reshape(-1, 8, 128)
     return jnp.concatenate([left, right], axis=1).astype(BF16)
 
 
@@ -65,9 +65,9 @@
     new_bank, losses, direction,
     pas_a, pas_b, w_a, w_b, acc,
     v_bank, v_touched, v_owner, v_row, v_q, v_pos, v_new, v_dir,
-    t1, r1, r1t, r2, sb0, sb1, rb0, rb1, rr0, rr1, fr0, fr1, fl0, fl1,
+    t0, t1, q0, q1, g0, g1, sb0, sb1, rr0, rr1, fr0, fr1, fl0, fl1,
     sel0, sel1, mat0, mat1, nb0, nb1, stats,
-    s_in, s_pas, s_own, w1s, w1r, w2s, w2r, qs, qr, as_, ar, fs, frs, gs, gr, s_out,
+    s_in, s_pas, s_own, w1s, w1r, w2s, w2r, bs, br, qs, qr, as_, ar, fs, frs, gs, gr, s_out,
 ):
     d = lax.axis_index("dev")
     g = lax.axis_index("grp")
@@ -92,6 +92,12 @@
     own_b = pltpu.make_async_copy(w.at[:, pl.ds(HALF, HALF)], w_b.at[z, y], s_own.at[1])
     own_a.start()
     own_b.start()
+    own_g = [
+        pltpu.make_async_copy(bank.at[:, pl.ds(0, HALF)], g0.at[y], s_own.at[2]),
+        pltpu.make_async_copy(bank.at[:, pl.ds(HALF, HALF)], g1.at[z], s_own.at[3]),
+    ]
+    for c in own_g:
+        c.start()
 
     barrier = pltpu.get_barrier_semaphore()
     for k in range(1, SIDE):
@@ -130,12 +136,15 @@
     own_col, row_col = column(v_owner), column(v_row)
     own_zy = own_col
     own_yz = lax.rem(own_col, SIDE) * SIDE + own_col // SIDE
-    named = ones(own_yz == iota((REQ, 128), 1))
+    named = ones(own_zy == iota((REQ, 128), 1))
     before = dot(ones(iota((REQ, REQ), 0) > iota((REQ, REQ), 1)), named)
     rank = jnp.sum(named.astype(F32) * before, axis=1, keepdims=True).astype(I32)
     entry = jnp.where(rank == iota((REQ, 128), 1), (row_col + 1).astype(F32), 0.0).astype(BF16)
-    table = lax.dot_general(named, entry, (((0,), (0,)), ((), ())), preferred_element_type=F32)
-    t1[...] = table[: SIDE * SIDE].reshape(SIDE, SIDE, 128)
+    for t, one in ((t0, named), (t1, ones(own_yz == iota((REQ, 128), 1)))):
+        table = lax.dot_general(one, entry, (((0,), (0,)), ((), ())), preferred_element_type=F32)
+        t[...] = table[: SIDE * SIDE].reshape(SIDE, SIDE, 128)
+    q0[pl.ds(z, 1)] = t0[pl.ds(z, 1)]
+    q1[pl.ds(y, 1)] = t1[pl.ds(y, 1)]
     pl.semaphore_wait(barrier, 2 * (SIDE - 1) + GRP - 1)
 
     def block(h, zz, yy):
@@ -183,16 +192,45 @@
 
     place = {1: 1, -1: 2, 2: 3, -2: 4, 3: 5, -3: 6, 4: 7}
 
-    r1[pl.ds(y, 1)] = t1[pl.ds(y, 1)]
-
-    def ask1(k):
-        return remote(t1.at[wrap(y + k)], r1.at[y], qs.at[k - 1], qr.at[k - 1], at(0, k))
-
-    def ask2(k):
-        return remote(r1t.at[wrap(z + k)], r2.at[z], qs.at[6 + k], qr.at[6 + k], at(k, 0))
-
-    for k in range(1, SIDE):
-        ask1(k).start()
+    def ask(h, k):
+        i = h * 7 + k - 1
+        if h == 0:
+            return remote(t0.at[wrap(z + k)], q0.at[z], qs.at[i], qr.at[i], at(k, 0))
+        return remote(t1.at[wrap(y + k)], q1.at[y], qs.at[i], qr.at[i], at(0, k))
+
+    def each(make, what):
+        for k in range(1, SIDE):
+            for h in range(2):
+                getattr(make(h, k), what)()
+
+    def shard(h, k, s, way):
+        b = g0.at[wrap(y + k)] if h == 0 else g1.at[wrap(z + k)]
+        return b if s < 4 else b.at[pl.ds(0 if way == 1 else 64, 64)]
+
+    def pass_bank(h, way, s):
+        i = (h * 2 + (1 - way) // 2) * 4 + s - 1
+        b = shard(h, -way * (s - 1), s, way)
+        src = bank.at[:, pl.ds(h * HALF, HALF)] if s == 1 else b
+        return remote(src, b, bs.at[i], br.at[i], along(1 - h, way))
+
+    def got_bank(s):
+        for h in range(2):
+            for way in (1, -1):
+                i = (h * 2 + (1 - way) // 2) * 4 + s - 1
+                b = shard(h, -way * s, s, way)
+                remote(b, b, bs.at[i], br.at[i], along(1 - h, way)).wait_recv()
+
+    def send_bank(s):
+        for h in range(2):
+            for way in (1, -1):
+                pass_bank(h, way, s).start()
+
+    def bank_on(s):
+        got_bank(s)
+        send_bank(s + 1)
+
+    send_bank(1)
+    each(ask, "start")
 
     for came in (1, -1):
         for h in range(2):
@@ -213,16 +251,6 @@
             got_first(h, came)
             for way in (1, -1):
                 second(h, way, 1, place[came]).start()
-
-    def ask_on():
-        for k in range(1, SIDE):
-            ask1(k).wait_recv()
-        zy = iota((64, 64), 0)
-        swap = ones(lax.rem(zy, SIDE) * SIDE + zy // SIDE == iota((64, 64), 1))
-        r1t[...] = dot(swap, r1[...].reshape(64, 128).astype(BF16)).reshape(SIDE, SIDE, 128)
-        r2[pl.ds(z, 1)] = r1t[pl.ds(z, 1)]
-        for k in range(1, SIDE):
-            ask2(k).start()
 
     def masks(h, own_pos, sel, mat, nb):
         ids = v_touched[...].reshape(1, NPAS * 64)
@@ -241,37 +269,31 @@
         sel[...] = ones((slot == iota((REQ, SLOTS), 1)) & (some < 0.5))
         nb[...] = ones((hi == d) & (lo == iota((BANK, NPAS * 64), 0)))
 
-    def answer(h, sb):
-        p = iota((SLOTS, 1), 0) // 8
-        asker = lax.rem(p, SIDE) * SIDE + p // SIDE if h == 0 else p
-        lines = dot(ones(asker == iota((SLOTS, 64), 1)), r2[...].reshape(64, 128).astype(BF16))
-        own = lax.rem(iota((SLOTS, 128), 0), 8) == iota((SLOTS, 128), 1)
+    def answer(h, q, held, sb):
+        p = iota((SLOTS, 1), 0) // CAP
+        asked = lax.rem(p, SIDE) * SIDE + p // SIDE
+        lines = dot(ones(asked == iota((SLOTS, 64), 1)), q[...].reshape(64, 128).astype(BF16))
+        own = lax.rem(iota((SLOTS, 128), 0), CAP) == iota((SLOTS, 128), 1)
         want = jnp.sum(jnp.where(own, lines, 0.0), axis=1, keepdims=True).astype(I32)
         pick = ones(want == iota((SLOTS, BANK), 1) + 1)
-        out = dot(pick, v_bank[:, h * HALF : (h + 1) * HALF])
-        sb[...] = spread(out).reshape(SIDE, SIDE, 16, 128)
-
-    def answer_0():
-        for k in range(1, SIDE):
-            ask2(k).wait_recv()
-        answer(0, sb0)
-        rb0[pl.ds(y, 1)] = sb0[pl.ds(y, 1)]
-
-    def answer_1():
-        answer(1, sb1)
-        rb1[pl.ds(z, 1)] = sb1[pl.ds(z, 1)]
-
-    def rows1(h, k):
+        for o in range(SIDE):
+            sb[:, o] = spread(dot(pick[o * 64 : (o + 1) * 64], held[o]))
+
+    def answers():
+        got_bank(4)
+        each(ask, "wait_recv")
+        for c in own_g:
+            c.wait()
+        answer(0, q0, g0, sb0)
+        answer(1, q1, g1, sb1)
+        rr0[pl.ds(z, 1)] = sb0[pl.ds(z, 1)]
+        rr1[pl.ds(y, 1)] = sb1[pl.ds(y, 1)]
+
+    def replies(h, k):
         i = h * 7 + k - 1
         if h == 0:
-            return remote(sb0.at[wrap(y + k)], rb0.at[y], as_.at[i], ar.at[i], at(0, k))
-        return remote(sb1.at[wrap(z + k)], rb1.at[z], as_.at[i], ar.at[i], at(k, 0))
-
-    def rows2(h, k):
-        i = 14 + h * 7 + k - 1
-        if h == 0:
-            return remote(rb0.at[:, wrap(z + k)], rr0.at[z], as_.at[i], ar.at[i], at(k, 0))
-        return remote(rb1.at[:, wrap(y + k)], rr1.at[y], as_.at[i], ar.at[i], at(0, k))
+            return remote(sb0.at[wrap(z + k)], rr0.at[z], as_.at[i], ar.at[i], at(k, 0))
+        return remote(sb1.at[wrap(y + k)], rr1.at[y], as_.at[i], ar.at[i], at(0, k))
 
     def loaded_b(k):
         load_b(k).wait()
@@ -319,11 +341,9 @@
     for c in loads[2:4]:
         c.wait()
     between = {
-        0: ask_on,
-        1: lambda: masks(0, own_zy, sel0, mat0, nb0),
-        3: lambda: masks(1, own_yz, sel1, mat1, nb1),
-        5: answer_0,
-        7: answer_1,
+        2: lambda: masks(0, own_zy, sel0, mat0, nb0),
+        7: lambda: bank_on(1),
+        5: lambda: masks(1, own_yz, sel1, mat1, nb1),
     }
     for j in range(SIDE):
         received(1, j, (1, -1))
@@ -337,13 +357,12 @@
     loaded_b(-1)
     loaded_a(pairs[0])
     ring_step(2, 0)
+    bank_on(2)
     loaded_b(2)
     loaded_b(-2)
     loaded_a(pairs[1])
     ring_step(3, 1)
-    for h in range(2):
-        for k in range(1, SIDE):
-            rows1(h, k).start()
+    bank_on(3)
     loaded_b(3)
     loaded_b(-3)
     loaded_a(pairs[2])
@@ -379,25 +398,18 @@
             return remote(fl0.at[z], fl0.at[z], fs.at[i], frs.at[i], at(k, 0))
         return remote(fl1.at[y], fl1.at[y], fs.at[i], frs.at[i], at(0, k))
 
-    def each(make, what):
-        for k in range(1, SIDE):
-            for h in range(2):
-                getattr(make(h, k), what)()
-
     each(fresh1, "start")
-    each(rows1, "wait_recv")
-    each(rows2, "start")
+    answers()
+    each(replies, "start")
     each(fresh1, "wait_recv")
     kept = iota((SIDE * NPAS, 1), 0)
     keep = ones(kept // NPAS * 8 + lax.rem(kept, NPAS) == iota((SIDE * NPAS, 64), 1))
     fl0[pl.ds(z, 1)] = dot(keep, joined(fr0[...])).astype(BF16).reshape(1, SIDE * NPAS, HALF)
     fl1[pl.ds(y, 1)] = dot(keep, joined(fr1[...])).astype(BF16).reshape(1, SIDE * NPAS, HALF)
     each(fresh2, "start")
-    rr0[pl.ds(z, 1)] = rb0[:, pl.ds(z, 1)].reshape(1, SIDE, 16, 128)
-    rr1[pl.ds(y, 1)] = rb1[:, pl.ds(y, 1)].reshape(1, SIDE, 16, 128)
     loads[4].wait()
     loads[5].wait()
-    each(rows2, "wait_recv")
+    each(replies, "wait_recv")
     old = [dot(m[...], joined(r[...].reshape(64, 16, 128))) for m, r in ((sel0, rr0), (sel1, rr1))]
     each(fresh2, "wait_recv")
     fresh = [f[...].reshape(NPAS * 64, HALF) for f in (fl0, fl1)]
@@ -461,10 +473,11 @@
             for s in range(1, 5):
                 sent = w_b.at[0] if s < 4 else w_b.at[0, pl.ds(0, 4)]
                 pltpu.make_async_copy(sent, sent, w2s.at[(h * 2 + way) * 4 + s - 1]).wait()
-    for k in range(1, SIDE):
-        ask1(k).wait_send()
-        ask2(k).wait_send()
-    for make in (rows1, rows2, fresh1, fresh2):
+    for h in range(2):
+        for way in (1, -1):
+            for s in range(1, 5):
+                pass_bank(h, way, s).wait_send()
+    for make in (ask, replies, fresh1, fresh2):
         each(make, "wait_send")
     for k in range(1, GRP):
         share(k).wait_send()
@@ -508,7 +521,8 @@
             V((BANK, COLS), BF16),
             V((QD, COLS), F32),
             *[V((SIDE, SIDE, 128), F32)] * 4,
-            *[slots] * 6,
+            *[V((SIDE, BANK, HALF), BF16)] * 2,
+            *[slots] * 4,
             *[V((SIDE, 16, 128), BF16)] * 2,
             *[V((SIDE, SIDE * NPAS, HALF), BF16)] * 2,
             *[V((REQ, SLOTS), BF16)] * 2,
@@ -517,15 +531,17 @@
             V((GRP, 8, 128), F32),
             dma((6,)),
             dma((12,)),
-            dma((2,)),
+            dma((4,)),
             dma((14,)),
             dma((14,)),
             dma((16,)),
             dma((16, 8)),
+            dma((16,)),
+            dma((16,)),
             dma((14,)),
             dma((14,)),
-            dma((28,)),
-            dma((28,)),
+            dma((14,)),
+            dma((14,)),
             dma((28,)),
             dma((28,)),
             dma((7,)),

time: 75 us -> 74.2 us (0.989)
  Pallas kernels: 74.2 us -> 73.4 us
    pallas_call x1, Pallas kernels: 72.6 us -> 71.8 us  [body(): pl.pallas_call(kernel, out_shape=(jax.ShapeDtypeStruct((BANK, COLS), BF16...]
where the time goes in v3:
time: 74.2 us; the launch traced here: 74 us
  Pallas kernels  73.4 us (99%)
    pallas_call x1, Pallas kernels, body(): pl.pallas_call(kernel, out_shape=(jax.ShapeDtypeStruct((BANK, COLS), BF16...  71.8 us
    pallas_call x1, Pallas kernels, body(): pl.pallas_call(place, out_shape=tuple((jax.ShapeDtypeStruct(r.shape, r.dt...  1.59 us

profile of v3, /device:TPU:1, one launch (start us, length us, event | category | flops | bytes accessed | tf_op | source)
XLA Modules:
  0.0 74.0 jit_solution(4242859113702594946)
XLA Ops:
  0.6 71.8 %shard_map.103 = (bf16[128,512]{1,0:T(8,128)(2,1)}, f32[1,32]{1,0:T(1,128)}, f32[32,512]{1,0:T(8,128)}) custom-call(bf16[1536,4096]{1,0:T(8,128)(2,1)} %pas.1, bf16[64,512]{1,0:T(8,128)(2,1)} %w.1, bf16[128,512]{1,0:T(8,128)(2,1)} %bank.1, s32[384]{0:T(512)} %touched.1, s32[8,32]{1,0:T(8,128)} %bitcast.3, s32[8,32]{1,0:T(8,128)} %bitcast.4, ...), custom_call_target="tpu_custom_call" | custom-call | tf_op jit(solution)/shard_map/pallas_call | solution.py:500
  72.4 1.6 %shard_map.104 = (bf16[128,512]{1,0:T(8,128)(2,1)}, f32[1,32]{1,0:T(1,128)}, f32[32,512]{1,0:T(8,128)}) custom-call(bf16[128,512]{1,0:T(8,128)(2,1)} %get-tuple-element.9.a, f32[1,32]{1,0:T(1,128)} %get-tuple-element.10.b, f32[32,512]{1,0:T(8,128)} %get-tuple-element.11.c), custom_call_target="tpu_custom_call" | custom-call | tf_op jit(solution)/shard_map/pallas_call | solution.py:556
